TPU v7x, 32 devices: a whole 2x2x4 slice. The times are simulated.
32 devices in a mesh: roll: 4 (over x, core), tp: 8 (over z, y).
Axes of the slice: x: 2, y: 2, z: 4, core: 2. Of those that a mesh axis runs over, the one named last changes fastest.
Arguments:
- tokens: bfloat16 [128, 8, 2048], P(('roll', 'tp')), may hold values from -6 to 6
- lengths: int32 [128], P(('roll', 'tp')), may hold values from 1 to 8
- plan: int32 [2, 128, 1], P(None, ('roll', 'tp')), may hold values from 0 to 3, as said below
- owners: int32 [4], replicated, may hold values from 0 to 3, each once
- gate_up: float32 [4, 8, 2048, 768], P('roll', 'tp'), may hold values from -0.125 to 0.125
- down: float32 [4, 8, 384, 2048], P('roll', 'tp'), may hold values from -0.3125 to 0.3125
- norm_gain: float32 [2, 2048], replicated, may hold values from 0.5 to 1.5
- routing: int32 [2, 2048, 1], P(None, ('roll', 'tp')), may hold values from 0 to 7; in each aligned block of 64 rows (0 to 63, 64 to 127, ..., all dimensions but the last counted through in order) at most 10 rows name the same one
- route_weight: float32 [2, 2048], P(None, ('roll', 'tp')), may hold values from 0.1 to 1
Outputs:
- result: bfloat16 [128, 8, 2048], P(('roll', 'tp'))
Inputs may be any that keep to these rules, and one draw needn't show every extreme that they name: In layer 0 at most 2 rows of one device name the same owner, and every device's rows reach 2. For l >= 1, plan[l, i, 0] = (r + s_l[plan[l - 1, i, 0]]) mod 4, with r the roll index of row i's device and s_l a permutation of the owners drawn for layer l. owners is a permutation; layer l's master lies in the slot of roll index owners[l]. `routing`: every received token slot, empty ones included, names one window expert; of the 64 slots of one device at most 10 name the same expert, and in every draw some device reaches 10.
All inputs are finite; a program needn't handle non-finite values.
Results may differ from a plain program's by a relative error of at most 0.0048.
Values may be sent and summed in bfloat16 or wider, within the bound.
A program may use at most 128 MiB of HBM per device.

v0:
```python
import jax
import jax.numpy as jnp
from jax import lax
from jax.sharding import PartitionSpec as P

CAP = 2
epsilon = 1e-06


def spread(block, axis, owner):
    block = jnp.where(lax.axis_index(axis) == owner, block, jnp.zeros_like(block))
    return lax.psum(block, axis)


def slot_plan(target, groups, capacity):
    onehot = (target[:, None] == jnp.arange(groups, dtype=jnp.int32)[None, :]).astype(jnp.int32)
    before = jnp.cumsum(onehot, axis=0) - onehot
    within = jnp.sum(before * onehot, axis=1)
    target_slot = target * capacity + within
    item_count = target.shape[0]
    source = (
        jnp.zeros((groups * capacity,), jnp.int32)
        .at[target_slot]
        .set(jnp.arange(item_count, dtype=jnp.int32))
    )
    filled = jnp.zeros((groups * capacity,), jnp.bool_).at[target_slot].set(True)
    return (target_slot, source, filled)


def fetch_layer(gate_up, down, owners, layer_index):
    local_slot = (gate_up[0, 0].astype(jnp.bfloat16), down[0, 0].astype(jnp.bfloat16))
    return (
        spread(local_slot[0], "roll", owners[layer_index]),
        spread(local_slot[1], "roll", owners[layer_index]),
    )


def send_rows_out(current, meta_rows, source, filled, roll_size):
    row_tokens = current.shape[1]
    model_width = current.shape[2]
    send_rows = jnp.where(filled[:, None, None], current[source], jnp.zeros((), current.dtype))
    send_rows = send_rows.reshape(roll_size, CAP, row_tokens, model_width)
    send_meta = jnp.where(filled[:, None], meta_rows[source], -1)
    send_meta = send_meta.reshape(roll_size, CAP, meta_rows.shape[1])
    got_rows, got_meta = (
        lax.all_to_all(send_rows, "roll", split_axis=0, concat_axis=0, tiled=True),
        lax.all_to_all(send_meta, "roll", split_axis=0, concat_axis=0, tiled=True),
    )
    return (got_rows.reshape(-1, row_tokens, model_width), got_meta.reshape(-1, meta_rows.shape[1]))


def send_home(combined, target_slot, roll_size):
    row_tokens = combined.shape[1]
    model_width = combined.shape[2]
    home_rows = lax.all_to_all(
        combined.reshape(roll_size, CAP, row_tokens, model_width),
        "roll",
        split_axis=0,
        concat_axis=0,
        tiled=True,
    )
    return home_rows.reshape(roll_size * CAP, row_tokens, model_width)[target_slot]


def process_rows(held, held_lengths, weights, layer_gain, route_column, weight_column):
    tp_size = lax.axis_size("tp")
    row_tokens = held.shape[1]
    model_width = held.shape[2]
    received = held.reshape(-1, model_width)
    token_count = received.shape[0]
    present = (jnp.arange(row_tokens)[None, :] < held_lengths[:, None]).reshape(-1)
    widened = received.astype(jnp.float32)
    normed = (
        widened
        * lax.rsqrt(jnp.mean(widened * widened, axis=1, keepdims=True) + epsilon)
        * layer_gain[None, :]
    ).astype(jnp.bfloat16)
    expert_slots = 5 * token_count // (4 * tp_size)
    expert_target, expert_source, expert_filled = slot_plan(route_column, tp_size, expert_slots)
    send_tokens = jnp.where(
        expert_filled[:, None], normed[expert_source], jnp.zeros((), normed.dtype)
    )
    send_tokens = send_tokens.reshape(tp_size, expert_slots, model_width)
    gate_up_w, down_w = weights
    hidden_width = down_w.shape[0]
    arrived = lax.all_to_all(send_tokens, "tp", split_axis=0, concat_axis=0, tiled=True)
    flattened = arrived.reshape(-1, model_width)
    projected = jnp.dot(flattened, gate_up_w, preferred_element_type=jnp.float32)
    hidden = (jax.nn.silu(projected[:, :hidden_width]) * projected[:, hidden_width:]).astype(
        jnp.bfloat16
    )
    produced = jnp.dot(hidden, down_w, preferred_element_type=jnp.float32).astype(jnp.bfloat16)
    returned = lax.all_to_all(
        produced.reshape(arrived.shape), "tp", split_axis=0, concat_axis=0, tiled=True
    )
    answer = returned.reshape(-1, model_width)[expert_target]
    combined = (
        widened
        + (present.astype(jnp.float32) * weight_column)[:, None] * answer.astype(jnp.float32)
    ).astype(jnp.bfloat16)
    return combined.reshape(held.shape)


def per_device(tokens, lengths, plan, owners, gate_up, down, norm_gain, routing, route_weight):
    layer_count = plan.shape[0]
    roll_size = lax.axis_size("roll")
    plans = [
        slot_plan(plan[layer_index, :, 0], roll_size, CAP) for layer_index in range(layer_count)
    ]
    current = tokens
    for layer_index in range(layer_count):
        held, held_meta = send_rows_out(
            current, lengths[:, None], plans[layer_index][1], plans[layer_index][2], roll_size
        )
        combined = process_rows(
            held,
            held_meta[:, 0],
            fetch_layer(gate_up, down, owners, layer_index),
            norm_gain[layer_index],
            routing[layer_index, :, 0],
            route_weight[layer_index],
        )
        current = send_home(combined, plans[layer_index][0], roll_size)
    return current


def solution(mesh):
    in_specs = (
        P(("roll", "tp"), None, None),
        P(("roll", "tp")),
        P(None, ("roll", "tp"), None),
        P(),
        P("roll", "tp", None, None),
        P("roll", "tp", None, None),
        P(),
        P(None, ("roll", "tp"), None),
        P(None, ("roll", "tp")),
    )
    out_specs = P(("roll", "tp"), None, None)
    return jax.shard_map(
        per_device, mesh=mesh, in_specs=in_specs, out_specs=out_specs, check_vma=False
    )
```

profile of v0, /device:TPU:0, one launch (start us, length us, event | category | flops | bytes accessed | tf_op | source)
XLA Modules:
  0.0 311.0 jit_solution(11454669175080193429)
XLA Ops:
  6.5 1.4 fusion.41
  9.3 3.9 %select_bitcast_fusion.3 = (bf16[384,2048]{1,0:T(8,128)(2,1)}, bf16[384,2048]{1,0:T(8,128)(2,1)}) fusion(pred[]{:T(512)S(6)} %eq.80, f32[1,1,384,2048]{3,2,1,0:T(8,128)} %param.14, pred[]{:T(512)S(6)} %eq.85), kind=kLoop, calls=%fused_computation.23 | loop fusion | flops 2359296 | bytes 6291458 | tf_op jit(solution)/shard_map/jit(_where)/select_n | solution.py:11
  13.2 0.9 copy-done.2
  14.1 3.1 select_bitcast_fusion
  21.0 4.2 %all-to-all-start = ((bf16[4,2,8,2048]{3,2,1,0:T(8,128)(2,1)}), bf16[4,2,8,2048]{3,2,1,0:T(8,128)(2,1)S(1)}, u32[]{:S(2)}, u32[]{:S(2)}) async-start(bf16[4,2,8,2048]{3,2,1,0:T(8,128)(2,1)} %broadcast_select_fusion.2), calls=%async_computation | async-start | bytes 524288 | tf_op jit(solution)/shard_map/all_to_all | solution.py:46
  27.5 6.7 %all-to-all-done = bf16[4,2,8,2048]{3,2,1,0:T(8,128)(2,1)S(1)} async-done(((bf16[4,2,8,2048]{3,2,1,0:T(8,128)(2,1)}), bf16[4,2,8,2048]{3,2,1,0:T(8,128)(2,1)S(1)}, u32[]{:S(2)}, u32[]{:S(2)}) %all-to-all-start) | async-done | bytes 262176 | tf_op jit(solution)/shard_map/all_to_all | solution.py:46
  36.4 6.6 %all-to-all-start.2 = ((bf16[8,10,2048]{2,1,0:T(8,128)(2,1)}), bf16[8,10,2048]{2,1,0:T(8,128)(2,1)S(1)}, u32[]{:S(2)}, u32[]{:S(2)}) async-start(bf16[8,10,2048]{2,1,0:T(8,128)(2,1)} %broadcast_select_fusion.1), calls=%async_computation.2 | async-start | bytes 1048576 | tf_op jit(solution)/shard_map/all_to_all | solution.py:86
  44.4 13.0 %all-to-all-done.2 = bf16[8,10,2048]{2,1,0:T(8,128)(2,1)S(1)} async-done(((bf16[8,10,2048]{2,1,0:T(8,128)(2,1)}), bf16[8,10,2048]{2,1,0:T(8,128)(2,1)S(1)}, u32[]{:S(2)}, u32[]{:S(2)}) %all-to-all-start.2) | async-done | bytes 327712 | tf_op jit(solution)/shard_map/all_to_all | solution.py:86
  57.4 3.2 %all-to-all-start.1 = ((s32[4,2,1]{1,2,0:T(1,128)}), s32[4,2,1]{1,2,0:T(1,128)S(1)}, u32[]{:S(2)}, u32[]{:S(2)}) async-start(s32[4,2,1]{1,2,0:T(1,128)} %bitcast.9), calls=%async_computation.1 | async-start | bytes 4096 | tf_op jit(solution)/shard_map/all_to_all | solution.py:47
  60.7 133.1 %all-reduce.3.cloned.1.call-done = (bf16[384,2048]{1,0:T(8,128)(2,1)}, bf16[384,2048]{1,0:T(8,128)(2,1)}, bf16[2048,768]{1,0:T(8,128)(2,1)}, bf16[2048,768]{1,0:T(8,128)(2,1)}) async-done(((bf16[384,2048]{1,0:T(8,128)(2,1)}, bf16[384,2048]{1,0:T(8,128)(2,1)}, bf16[2048,768]{1,0:T(8,128)(2,1)}, bf16[2048,768]{1,0:T(8,128)(2,1)}), (bf16[384,2048]{1,0:T(8,128)(2,1)}, bf16[384,2048]{1,0:T(8,128)(2,1)}, ...) | async-done | bytes 9437200 | tf_op jit(solution)/shard_map/psum | solution.py:12
  193.8 2.7 fusion.42
  196.9 0.9 reshape.292
  197.8 5.5 %all-to-all-start.3 = ((bf16[8,10,2048]{2,1,0:T(8,128)(2,1)}), bf16[8,10,2048]{2,1,0:T(8,128)(2,1)S(1)}, u32[]{:S(2)}, u32[]{:S(2)}) async-start(bf16[8,10,2048]{2,1,0:T(8,128)(2,1)} %reshape.292), calls=%async_computation.3 | async-start | bytes 1048576 | tf_op jit(solution)/shard_map/all_to_all | solution.py:93
  206.2 11.5 %all-to-all-done.3 = bf16[8,10,2048]{2,1,0:T(8,128)(2,1)S(1)} async-done(((bf16[8,10,2048]{2,1,0:T(8,128)(2,1)}), bf16[8,10,2048]{2,1,0:T(8,128)(2,1)S(1)}, u32[]{:S(2)}, u32[]{:S(2)}) %all-to-all-start.3) | async-done | bytes 327712 | tf_op jit(solution)/shard_map/all_to_all | solution.py:93
  219.4 3.4 %all-to-all-start.4 = ((bf16[4,2,8,2048]{3,2,1,0:T(8,128)(2,1)}), bf16[4,2,8,2048]{3,2,1,0:T(8,128)(2,1)S(1)}, u32[]{:S(2)}, u32[]{:S(2)}) async-start(bf16[4,2,8,2048]{3,2,1,0:T(8,128)(2,1)} %fusion.3), calls=%async_computation.4 | async-start | bytes 524288 | tf_op jit(solution)/shard_map/all_to_all | solution.py:55
  222.9 6.0 %all-to-all-done.4 = bf16[4,2,8,2048]{3,2,1,0:T(8,128)(2,1)S(1)} async-done(((bf16[4,2,8,2048]{3,2,1,0:T(8,128)(2,1)}), bf16[4,2,8,2048]{3,2,1,0:T(8,128)(2,1)S(1)}, u32[]{:S(2)}, u32[]{:S(2)}) %all-to-all-start.4) | async-done | bytes 262176 | tf_op jit(solution)/shard_map/all_to_all | solution.py:55
  230.8 3.4 %all-to-all-start.5 = ((bf16[4,2,8,2048]{3,2,1,0:T(8,128)(2,1)}), bf16[4,2,8,2048]{3,2,1,0:T(8,128)(2,1)S(1)}, u32[]{:S(2)}, u32[]{:S(2)}) async-start(bf16[4,2,8,2048]{3,2,1,0:T(8,128)(2,1)} %broadcast_select_fusion.3), calls=%async_computation.5 | async-start | bytes 524288 | tf_op jit(solution)/shard_map/all_to_all | solution.py:46
  235.6 4.5 %all-to-all-done.5 = bf16[4,2,8,2048]{3,2,1,0:T(8,128)(2,1)S(1)} async-done(((bf16[4,2,8,2048]{3,2,1,0:T(8,128)(2,1)}), bf16[4,2,8,2048]{3,2,1,0:T(8,128)(2,1)S(1)}, u32[]{:S(2)}, u32[]{:S(2)}) %all-to-all-start.5) | async-done | bytes 262176 | tf_op jit(solution)/shard_map/all_to_all | solution.py:46
  240.6 1.5 gather_fusion.7
  242.1 2.0 gather.55
  244.1 2.0 broadcast_select_fusion
  246.1 4.1 %all-to-all-start.7 = ((bf16[8,10,2048]{2,1,0:T(8,128)(2,1)}), bf16[8,10,2048]{2,1,0:T(8,128)(2,1)}, u32[]{:S(2)}, u32[]{:S(2)}) async-start(bf16[8,10,2048]{2,1,0:T(8,128)(2,1)} %broadcast_select_fusion), calls=%async_computation.7 | async-start | bytes 1048576 | tf_op jit(solution)/shard_map/all_to_all | solution.py:86
  250.2 1.2 gather_fusion.6
  252.7 12.1 %all-to-all-done.7 = bf16[8,10,2048]{2,1,0:T(8,128)(2,1)} async-done(((bf16[8,10,2048]{2,1,0:T(8,128)(2,1)}), bf16[8,10,2048]{2,1,0:T(8,128)(2,1)}, u32[]{:S(2)}, u32[]{:S(2)}) %all-to-all-start.7) | async-done | bytes 327712 | tf_op jit(solution)/shard_map/all_to_all | solution.py:86
  264.8 3.2 %all-to-all-start.6 = ((s32[4,2,1]{1,2,0:T(1,128)}), s32[4,2,1]{1,2,0:T(1,128)S(1)}, u32[]{:S(2)}, u32[]{:S(2)}) async-start(s32[4,2,1]{1,2,0:T(1,128)} %bitcast.23), calls=%async_computation.6 | async-start | bytes 4096 | tf_op jit(solution)/shard_map/all_to_all | solution.py:47
  268.0 1.9 reshape.296
  269.9 1.7 fusion.43
  273.0 3.6 %all-to-all-start.8 = ((bf16[8,10,2048]{2,1,0:T(8,128)(2,1)}), bf16[8,10,2048]{2,1,0:T(8,128)(2,1)S(1)}, u32[]{:S(2)}, u32[]{:S(2)}) async-start(bf16[8,10,2048]{2,1,0:T(8,128)(2,1)} %reshape.297), calls=%async_computation.8 | async-start | bytes 1048576 | tf_op jit(solution)/shard_map/all_to_all | solution.py:93
  276.8 15.0 %all-to-all-done.8 = bf16[8,10,2048]{2,1,0:T(8,128)(2,1)S(1)} async-done(((bf16[8,10,2048]{2,1,0:T(8,128)(2,1)}), bf16[8,10,2048]{2,1,0:T(8,128)(2,1)S(1)}, u32[]{:S(2)}, u32[]{:S(2)}) %all-to-all-start.8) | async-done | bytes 327712 | tf_op jit(solution)/shard_map/all_to_all | solution.py:93
  293.5 3.4 %all-to-all-start.9 = ((bf16[4,2,8,2048]{3,2,1,0:T(8,128)(2,1)}), bf16[4,2,8,2048]{3,2,1,0:T(8,128)(2,1)S(1)}, u32[]{:S(2)}, u32[]{:S(2)}) async-start(bf16[4,2,8,2048]{3,2,1,0:T(8,128)(2,1)} %fusion.1), calls=%async_computation.9 | async-start | bytes 524288 | tf_op jit(solution)/shard_map/all_to_all | solution.py:55
  296.9 6.0 %all-to-all-done.9 = bf16[4,2,8,2048]{3,2,1,0:T(8,128)(2,1)S(1)} async-done(((bf16[4,2,8,2048]{3,2,1,0:T(8,128)(2,1)}), bf16[4,2,8,2048]{3,2,1,0:T(8,128)(2,1)S(1)}, u32[]{:S(2)}, u32[]{:S(2)}) %all-to-all-start.9) | async-done | bytes 262176 | tf_op jit(solution)/shard_map/all_to_all | solution.py:55
  302.9 1.2 gather_fusion.9
  (108 shorter events, 22.8 us)
Async XLA Ops:
  6.5 13.1 %copy-start = (bf16[4,8,2048]{2,1,0:T(8,128)(2,1)S(1)}, bf16[4,8,2048]{2,1,0:T(8,128)(2,1)}, u32[]{:S(2)}) copy-start(bf16[4,8,2048]{2,1,0:T(8,128)(2,1)} %param.9) | copy-start | bytes 393220
  6.5 187.3 %all-reduce.3.cloned.1.call-start = ((), (), s32[]{:S(2)}) async-start(), calls=%async_computation.10 | async-start | bytes 18874368 | tf_op jit(solution)/shard_map/psum | solution.py:12
  9.3 4.9 %copy-start.2 = (f32[1,1,2048,768]{3,2,1,0:T(8,128)S(1)}, f32[1,1,2048,768]{3,2,1,0:T(8,128)}, u32[]{:S(2)}) copy-start(f32[1,1,2048,768]{3,2,1,0:T(8,128)} %param.13) | copy-start | bytes 18874372
  17.2 0.7 copy-start.7
  17.2 8.0 %copy-start.8 = (s32[2,64,1]{1,2,0:T(1,128)S(1)}, s32[2,64,1]{1,2,0:T(1,128)}, u32[]{:S(2)}) copy-start(s32[2,64,1]{1,2,0:T(1,128)} %param.16) | copy-start | bytes 1540
  17.2 9.4 %copy-start.6 = (f32[2,2048]{1,0:T(2,128)S(1)}, f32[2,2048]{1,0:T(2,128)}, u32[]{:S(2)}) copy-start(f32[2,2048]{1,0:T(2,128)} %param.15) | copy-start | bytes 49156
  21.0 13.2 %all-to-all-start = ((bf16[4,2,8,2048]{3,2,1,0:T(8,128)(2,1)}), bf16[4,2,8,2048]{3,2,1,0:T(8,128)(2,1)S(1)}, u32[]{:S(2)}, u32[]{:S(2)}) async-start(bf16[4,2,8,2048]{3,2,1,0:T(8,128)(2,1)} %broadcast_select_fusion.2), calls=%async_computation | async-start | bytes 524288 | tf_op jit(solution)/shard_map/all_to_all | solution.py:46
  34.5 8.5 %copy-start.1 = (s32[4]{0:T(128)S(1)}, s32[4]{0:T(128)}, u32[]{:S(2)}) copy-start(s32[4]{0:T(128)} %param.10) | copy-start | bytes 52
  36.4 20.9 %all-to-all-start.2 = ((bf16[8,10,2048]{2,1,0:T(8,128)(2,1)}), bf16[8,10,2048]{2,1,0:T(8,128)(2,1)S(1)}, u32[]{:S(2)}, u32[]{:S(2)}) async-start(bf16[8,10,2048]{2,1,0:T(8,128)(2,1)} %broadcast_select_fusion.1), calls=%async_computation.2 | async-start | bytes 1048576 | tf_op jit(solution)/shard_map/all_to_all | solution.py:86
  57.4 140.5 %all-to-all-start.1 = ((s32[4,2,1]{1,2,0:T(1,128)}), s32[4,2,1]{1,2,0:T(1,128)S(1)}, u32[]{:S(2)}, u32[]{:S(2)}) async-start(s32[4,2,1]{1,2,0:T(1,128)} %bitcast.9), calls=%async_computation.1 | async-start | bytes 4096 | tf_op jit(solution)/shard_map/all_to_all | solution.py:47
  193.8 2.7 copy-start.5
  193.8 9.5 %copy-start.10 = (f32[2,64]{1,0:T(2,128)S(1)}, f32[2,64]{1,0:T(2,128)}, u32[]{:S(2)}) copy-start(f32[2,64]{1,0:T(2,128)} %param.17) | copy-start | bytes 1540
  197.8 19.9 %all-to-all-start.3 = ((bf16[8,10,2048]{2,1,0:T(8,128)(2,1)}), bf16[8,10,2048]{2,1,0:T(8,128)(2,1)S(1)}, u32[]{:S(2)}, u32[]{:S(2)}) async-start(bf16[8,10,2048]{2,1,0:T(8,128)(2,1)} %reshape.292), calls=%async_computation.3 | async-start | bytes 1048576 | tf_op jit(solution)/shard_map/all_to_all | solution.py:93
  204.6 1.5 copy-start.11
  219.4 9.4 %all-to-all-start.4 = ((bf16[4,2,8,2048]{3,2,1,0:T(8,128)(2,1)}), bf16[4,2,8,2048]{3,2,1,0:T(8,128)(2,1)S(1)}, u32[]{:S(2)}, u32[]{:S(2)}) async-start(bf16[4,2,8,2048]{3,2,1,0:T(8,128)(2,1)} %fusion.3), calls=%async_computation.4 | async-start | bytes 524288 | tf_op jit(solution)/shard_map/all_to_all | solution.py:55
  230.8 9.4 %all-to-all-start.5 = ((bf16[4,2,8,2048]{3,2,1,0:T(8,128)(2,1)}), bf16[4,2,8,2048]{3,2,1,0:T(8,128)(2,1)S(1)}, u32[]{:S(2)}, u32[]{:S(2)}) async-start(bf16[4,2,8,2048]{3,2,1,0:T(8,128)(2,1)} %broadcast_select_fusion.3), calls=%async_computation.5 | async-start | bytes 524288 | tf_op jit(solution)/shard_map/all_to_all | solution.py:46
  242.1 27.8 %copy-start.3 = (bf16[2048,768]{1,0:T(8,128)(2,1)S(1)}, bf16[2048,768]{1,0:T(8,128)(2,1)}, u32[]{:S(2)}) copy-start(bf16[2048,768]{1,0:T(8,128)(2,1)} %get-tuple-element.10) | copy-start | bytes 9437188
  246.1 18.7 %all-to-all-start.7 = ((bf16[8,10,2048]{2,1,0:T(8,128)(2,1)}), bf16[8,10,2048]{2,1,0:T(8,128)(2,1)}, u32[]{:S(2)}, u32[]{:S(2)}) async-start(bf16[8,10,2048]{2,1,0:T(8,128)(2,1)} %broadcast_select_fusion), calls=%async_computation.7 | async-start | bytes 1048576 | tf_op jit(solution)/shard_map/all_to_all | solution.py:86
  264.8 8.2 %all-to-all-start.6 = ((s32[4,2,1]{1,2,0:T(1,128)}), s32[4,2,1]{1,2,0:T(1,128)S(1)}, u32[]{:S(2)}, u32[]{:S(2)}) async-start(s32[4,2,1]{1,2,0:T(1,128)} %bitcast.23), calls=%async_computation.6 | async-start | bytes 4096 | tf_op jit(solution)/shard_map/all_to_all | solution.py:47
  269.9 1.7 copy-start.4
  269.9 6.7 %copy-start.9 = (f32[64]{0:T(128)S(1)}, f32[64]{0:T(128)}, u32[]{:S(2)}) copy-start(f32[64]{0:T(128)} %get-tuple-element.5) | copy-start | bytes 772
  273.0 18.8 %all-to-all-start.8 = ((bf16[8,10,2048]{2,1,0:T(8,128)(2,1)}), bf16[8,10,2048]{2,1,0:T(8,128)(2,1)S(1)}, u32[]{:S(2)}, u32[]{:S(2)}) async-start(bf16[8,10,2048]{2,1,0:T(8,128)(2,1)} %reshape.297), calls=%async_computation.8 | async-start | bytes 1048576 | tf_op jit(solution)/shard_map/all_to_all | solution.py:93
  293.5 9.4 %all-to-all-start.9 = ((bf16[4,2,8,2048]{3,2,1,0:T(8,128)(2,1)}), bf16[4,2,8,2048]{3,2,1,0:T(8,128)(2,1)S(1)}, u32[]{:S(2)}, u32[]{:S(2)}) async-start(bf16[4,2,8,2048]{3,2,1,0:T(8,128)(2,1)} %fusion.1), calls=%async_computation.9 | async-start | bytes 524288 | tf_op jit(solution)/shard_map/all_to_all | solution.py:55
Sparse Core Ops, SparseCore 0:
  17.4 176.4 all-reduce.2
where the time goes:
time: 312 us; the launch traced here: 311 us
  waiting for transfers between devices  208 us (67%)
  starting transfers between devices  40.7 us (13%)
  local copies, waits for them, and re-layouts  26.3 us (8%)
  other arithmetic  15.6 us (5%)
  between operations  15.1 us (5%)
  matrix products  5.22 us (2%)
    psum x1, waiting for transfers between devices, spread(): return lax.psum(block, axis)  133 us
    all_to_all x2, waiting for transfers between devices, process_rows(): lax.all_to_all(produced.reshape(arrived.shape), 'tp', split_axis=0, conca...  26.5 us
    all_to_all x2, waiting for transfers between devices, process_rows(): lax.all_to_all(send_tokens, 'tp', split_axis=0, concat_axis=0, tiled=True)  25.1 us
    all_to_all x2, waiting for transfers between devices, send_home(): lax.all_to_all(combined.reshape(roll_size, CAP, row_tokens, model_width),...  12 us
    all_to_all x2, waiting for transfers between devices, send_rows_out(): lax.all_to_all(send_rows, 'roll', split_axis=0, concat_axis=0, tiled=True)  11.3 us
    all_to_all x2, starting transfers between devices, process_rows(): lax.all_to_all(send_tokens, 'tp', split_axis=0, concat_axis=0, tiled=True)  10.7 us
    all_to_all x2, starting transfers between devices, process_rows(): lax.all_to_all(produced.reshape(arrived.shape), 'tp', split_axis=0, conca...  9.14 us
    all_to_all x2, starting transfers between devices, send_rows_out(): lax.all_to_all(send_rows, 'roll', split_axis=0, concat_axis=0, tiled=True)  7.61 us
  transfers between devices with their start and end apart: 11, of which 9 were waited for; matrix products, arithmetic and copies ran while one was open for 8% of the time, Pallas kernels for 0%

commit v1 on v0

--- a/solution.py
+++ b/solution.py
@@ -9,7 +9,11 @@
 
 def spread(block, axis, owner):
     block = jnp.where(lax.axis_index(axis) == owner, block, jnp.zeros_like(block))
-    return lax.psum(block, axis)
+
+    def choose_shelves_for(message, shard_axis):
+        return lax.all_gather(message, axis_name=shard_axis).sum(axis=0)
+
+    return choose_shelves_for(block, axis)
 
 
 def slot_plan(target, groups, capacity):

time: 312 us -> 341 us (1.093)
  other arithmetic: 15.6 us -> 45.6 us
  local copies, waits for them, and re-layouts: 26.3 us -> 21.5 us
    all_gather x0 -> x4, waiting for transfers between devices: none -> 142 us  [choose_shelves_for(): return lax.all_gather(message, axis_name=shard_axis).sum(axis=0)]
    psum x1 -> x0, waiting for transfers between devices: 133 us -> none  [spread(): return lax.psum(block, axis)]
    reduce_sum x0 -> x4, other arithmetic: none -> 29.1 us  [choose_shelves_for(): return lax.all_gather(message, axis_name=shard_axis).sum(axis=0)]
    all_to_all x2, waiting for transfers between devices: 25.1 us -> 13 us  [process_rows(): lax.all_to_all(send_tokens, 'tp', split_axis=0, concat_axis=0, tiled=True)]
  transfers between devices with their start and end apart: 11 -> 14, of which waited for: 9 -> 10; matrix products, arithmetic and copies ran while one was open for 8% -> 19% of each run, Pallas kernels for 0% -> 0%
where the time goes in v1:
time: 341 us; the launch traced here: 340 us
  waiting for transfers between devices  211 us (62%)
  other arithmetic  45.6 us (13%)
  starting transfers between devices  42.6 us (12%)
  local copies, waits for them, and re-layouts  21.5 us (6%)
  between operations  14.9 us (4%)
  matrix products  4.34 us (1%)
    all_gather x4, waiting for transfers between devices, choose_shelves_for(): return lax.all_gather(message, axis_name=shard_axis).sum(axis=0)  142 us
    reduce_sum x4, other arithmetic, choose_shelves_for(): return lax.all_gather(message, axis_name=shard_axis).sum(axis=0)  29.1 us
    all_to_all x2, waiting for transfers between devices, process_rows(): lax.all_to_all(produced.reshape(arrived.shape), 'tp', split_axis=0, conca...  27.5 us
    all_to_all x2, waiting for transfers between devices, send_home(): lax.all_to_all(combined.reshape(roll_size, CAP, row_tokens, model_width),...  15.1 us
    all_to_all x2, waiting for transfers between devices, process_rows(): lax.all_to_all(send_tokens, 'tp', split_axis=0, concat_axis=0, tiled=True)  13 us
    all_to_all x2, waiting for transfers between devices, send_rows_out(): lax.all_to_all(send_rows, 'roll', split_axis=0, concat_axis=0, tiled=True)  11.9 us
    all_to_all x2, starting transfers between devices, process_rows(): lax.all_to_all(produced.reshape(arrived.shape), 'tp', split_axis=0, conca...  11 us
    all_to_all x2, starting transfers between devices, process_rows(): lax.all_to_all(send_tokens, 'tp', split_axis=0, concat_axis=0, tiled=True)  10.5 us
  transfers between devices with their start and end apart: 14, of which 10 were waited for; matrix products, arithmetic and copies ran while one was open for 19% of the time, Pallas kernels for 0%

profile of v1, /device:TPU:0, one launch (start us, length us, event | category | flops | bytes accessed | tf_op | source)
XLA Modules:
  0.0 339.6 jit_solution(15287888801577794617)
XLA Ops:
  6.5 1.4 fusion.41
  9.3 3.8 %broadcast_select_fusion.3 = (bf16[1,1,384,2048]{3,2,1,0:T(8,128)(2,1)}, bf16[1,1,384,2048]{3,2,1,0:T(8,128)(2,1)}) fusion(pred[]{:T(512)S(6)} %eq.80, f32[1,1,384,2048]{3,2,1,0:T(8,128)} %param.14, pred[]{:T(512)S(6)} %eq.85), kind=kLoop, calls=%fused_computation.23 | loop fusion | flops 2359296 | bytes 6291458 | tf_op jit(solution)/shard_map/jit(_where)/select_n | solution.py:11
  13.1 5.9 %broadcast_select_fusion = (bf16[1,1,2048,768]{3,2,1,0:T(8,128)(2,1)}, bf16[1,1,2048,768]{3,2,1,0:T(8,128)(2,1)}) fusion(pred[]{:T(512)S(6)} %eq.85, f32[1,1,2048,768]{3,2,1,0:T(8,128)} %param.13, pred[]{:T(512)S(6)} %eq.80), kind=kLoop, calls=%fused_computation.18 | loop fusion | flops 4718592 | bytes 12582914 | tf_op jit(solution)/shard_map/jit(_where)/select_n | solution.py:11
  23.5 4.2 %all-to-all-start = ((bf16[4,2,8,2048]{3,2,1,0:T(8,128)(2,1)}), bf16[4,2,8,2048]{3,2,1,0:T(8,128)(2,1)S(1)}, u32[]{:S(2)}, u32[]{:S(2)}) async-start(bf16[4,2,8,2048]{3,2,1,0:T(8,128)(2,1)} %broadcast_select_fusion.6), calls=%async_computation | async-start | bytes 524288 | tf_op jit(solution)/shard_map/all_to_all | solution.py:50
  30.0 6.9 %all-to-all-done = bf16[4,2,8,2048]{3,2,1,0:T(8,128)(2,1)S(1)} async-done(((bf16[4,2,8,2048]{3,2,1,0:T(8,128)(2,1)}), bf16[4,2,8,2048]{3,2,1,0:T(8,128)(2,1)S(1)}, u32[]{:S(2)}, u32[]{:S(2)}) %all-to-all-start) | async-done | bytes 262176 | tf_op jit(solution)/shard_map/all_to_all | solution.py:50
  39.2 6.4 %all-to-all-start.2 = ((bf16[8,10,2048]{2,1,0:T(8,128)(2,1)}), bf16[8,10,2048]{2,1,0:T(8,128)(2,1)S(1)}, u32[]{:S(2)}, u32[]{:S(2)}) async-start(bf16[8,10,2048]{2,1,0:T(8,128)(2,1)} %broadcast_select_fusion.5), calls=%async_computation.2 | async-start | bytes 1048576 | tf_op jit(solution)/shard_map/all_to_all | solution.py:90
  46.9 13.0 %all-to-all-done.2 = bf16[8,10,2048]{2,1,0:T(8,128)(2,1)S(1)} async-done(((bf16[8,10,2048]{2,1,0:T(8,128)(2,1)}), bf16[8,10,2048]{2,1,0:T(8,128)(2,1)S(1)}, u32[]{:S(2)}, u32[]{:S(2)}) %all-to-all-start.2) | async-done | bytes 327712 | tf_op jit(solution)/shard_map/all_to_all | solution.py:90
  59.9 3.2 all-to-all-start.1
  64.0 1.3 all-gather.11.cloned.1.call-done
  65.3 5.7 %reduce_sum.118 = bf16[384,2048]{1,0:T(8,128)(2,1)} reduce(bf16[4,1,384,2048]{3,2,1,0:T(8,128)(2,1)} %all-gather.11.cloned.1.call-done, bf16[]{:T(256)} %constant.55.clone.1), dimensions={0,1}, to_apply=%region_13.14 | reduce | flops 2359296 | bytes 7864322 | tf_op jit(solution)/shard_map/reduce_sum | solution.py:14
  71.0 78.0 %all-gather.9.cloned.1.call-done = bf16[4,1,2048,768]{3,2,1,0:T(8,128)(2,1)} async-done(((bf16[1,1,2048,768]{3,2,1,0:T(8,128)(2,1)}), bf16[4,1,2048,768]{3,2,1,0:T(8,128)(2,1)}) %all-gather.9.cloned.1.call-update) | async-done | bytes 12582928 | tf_op jit(solution)/shard_map/all_gather | solution.py:14
  149.0 8.6 %reduce_sum.117 = bf16[2048,768]{1,0:T(8,128)(2,1)S(1)} reduce(bf16[4,1,2048,768]{3,2,1,0:T(8,128)(2,1)} %all-gather.9.cloned.1.call-done, bf16[]{:T(256)} %constant.55.clone.1), dimensions={0,1}, to_apply=%region_12.13 | reduce | flops 4718592 | bytes 15728642 | tf_op jit(solution)/shard_map/reduce_sum | solution.py:14
  157.6 1.8 fusion.42
  160.7 5.5 %all-to-all-start.3 = ((bf16[8,10,2048]{2,1,0:T(8,128)(2,1)}), bf16[8,10,2048]{2,1,0:T(8,128)(2,1)S(1)}, u32[]{:S(2)}, u32[]{:S(2)}) async-start(bf16[8,10,2048]{2,1,0:T(8,128)(2,1)} %reshape.332), calls=%async_computation.3 | async-start | bytes 1048576 | tf_op jit(solution)/shard_map/all_to_all | solution.py:97
  168.6 12.5 %all-to-all-done.3 = bf16[8,10,2048]{2,1,0:T(8,128)(2,1)S(1)} async-done(((bf16[8,10,2048]{2,1,0:T(8,128)(2,1)}), bf16[8,10,2048]{2,1,0:T(8,128)(2,1)S(1)}, u32[]{:S(2)}, u32[]{:S(2)}) %all-to-all-start.3) | async-done | bytes 327712 | tf_op jit(solution)/shard_map/all_to_all | solution.py:97
  182.8 3.4 %all-to-all-start.4 = ((bf16[4,2,8,2048]{3,2,1,0:T(8,128)(2,1)}), bf16[4,2,8,2048]{3,2,1,0:T(8,128)(2,1)S(1)}, u32[]{:S(2)}, u32[]{:S(2)}) async-start(bf16[4,2,8,2048]{3,2,1,0:T(8,128)(2,1)} %fusion.3), calls=%async_computation.4 | async-start | bytes 524288 | tf_op jit(solution)/shard_map/all_to_all | solution.py:59
  186.3 9.1 %all-to-all-done.4 = bf16[4,2,8,2048]{3,2,1,0:T(8,128)(2,1)S(1)} async-done(((bf16[4,2,8,2048]{3,2,1,0:T(8,128)(2,1)}), bf16[4,2,8,2048]{3,2,1,0:T(8,128)(2,1)S(1)}, u32[]{:S(2)}, u32[]{:S(2)}) %all-to-all-start.4) | async-done | bytes 262176 | tf_op jit(solution)/shard_map/all_to_all | solution.py:59
  197.3 3.4 %all-to-all-start.5 = ((bf16[4,2,8,2048]{3,2,1,0:T(8,128)(2,1)}), bf16[4,2,8,2048]{3,2,1,0:T(8,128)(2,1)S(1)}, u32[]{:S(2)}, u32[]{:S(2)}) async-start(bf16[4,2,8,2048]{3,2,1,0:T(8,128)(2,1)} %broadcast_select_fusion.7), calls=%async_computation.5 | async-start | bytes 524288 | tf_op jit(solution)/shard_map/all_to_all | solution.py:50
  200.7 1.0 scatter_custom_fusion.6
  201.8 4.9 %all-to-all-done.5 = bf16[4,2,8,2048]{3,2,1,0:T(8,128)(2,1)S(1)} async-done(((bf16[4,2,8,2048]{3,2,1,0:T(8,128)(2,1)}), bf16[4,2,8,2048]{3,2,1,0:T(8,128)(2,1)S(1)}, u32[]{:S(2)}, u32[]{:S(2)}) %all-to-all-start.5) | async-done | bytes 262176 | tf_op jit(solution)/shard_map/all_to_all | solution.py:50
  208.9 4.1 %all-to-all-start.7 = ((bf16[8,10,2048]{2,1,0:T(8,128)(2,1)}), bf16[8,10,2048]{2,1,0:T(8,128)(2,1)}, u32[]{:S(2)}, u32[]{:S(2)}) async-start(bf16[8,10,2048]{2,1,0:T(8,128)(2,1)} %broadcast_select_fusion.4), calls=%async_computation.7 | async-start | bytes 1048576 | tf_op jit(solution)/shard_map/all_to_all | solution.py:90
  214.4 6.2 %reduce_sum.123 = bf16[384,2048]{1,0:T(8,128)(2,1)} reduce(bf16[4,1,384,2048]{3,2,1,0:T(8,128)(2,1)} %all-gather.15.cloned.1.call-done, bf16[]{:T(256)} %constant.55.clone.1), dimensions={0,1}, to_apply=%region_21.22 | reduce | flops 2359296 | bytes 7864322 | tf_op jit(solution)/shard_map/reduce_sum | solution.py:14
  220.6 62.7 %all-gather.13.cloned.1.call-done = bf16[4,1,2048,768]{3,2,1,0:T(8,128)(2,1)} async-done(((bf16[1,1,2048,768]{3,2,1,0:T(8,128)(2,1)}), bf16[4,1,2048,768]{3,2,1,0:T(8,128)(2,1)}) %all-gather.13.cloned.1.call-update) | async-done | bytes 12582928 | tf_op jit(solution)/shard_map/all_gather | solution.py:14
  283.3 8.6 %reduce_sum.122 = bf16[2048,768]{1,0:T(8,128)(2,1)S(1)} reduce(bf16[4,1,2048,768]{3,2,1,0:T(8,128)(2,1)} %all-gather.13.cloned.1.call-done, bf16[]{:T(256)} %constant.55.clone.1), dimensions={0,1}, to_apply=%region_20.21 | reduce | flops 4718592 | bytes 15728642 | tf_op jit(solution)/shard_map/reduce_sum | solution.py:14
  291.9 3.2 all-to-all-start.6
  295.2 1.9 reshape.336
  297.0 1.7 fusion.43
  300.1 5.5 %all-to-all-start.8 = ((bf16[8,10,2048]{2,1,0:T(8,128)(2,1)}), bf16[8,10,2048]{2,1,0:T(8,128)(2,1)S(1)}, u32[]{:S(2)}, u32[]{:S(2)}) async-start(bf16[8,10,2048]{2,1,0:T(8,128)(2,1)} %reshape.337), calls=%async_computation.8 | async-start | bytes 1048576 | tf_op jit(solution)/shard_map/all_to_all | solution.py:97
  305.8 15.0 %all-to-all-done.8 = bf16[8,10,2048]{2,1,0:T(8,128)(2,1)S(1)} async-done(((bf16[8,10,2048]{2,1,0:T(8,128)(2,1)}), bf16[8,10,2048]{2,1,0:T(8,128)(2,1)S(1)}, u32[]{:S(2)}, u32[]{:S(2)}) %all-to-all-start.8) | async-done | bytes 327712 | tf_op jit(solution)/shard_map/all_to_all | solution.py:97
  322.5 3.4 %all-to-all-start.9 = ((bf16[4,2,8,2048]{3,2,1,0:T(8,128)(2,1)}), bf16[4,2,8,2048]{3,2,1,0:T(8,128)(2,1)S(1)}, u32[]{:S(2)}, u32[]{:S(2)}) async-start(bf16[4,2,8,2048]{3,2,1,0:T(8,128)(2,1)} %fusion.1), calls=%async_computation.9 | async-start | bytes 524288 | tf_op jit(solution)/shard_map/all_to_all | solution.py:59
  325.9 6.0 %all-to-all-done.9 = bf16[4,2,8,2048]{3,2,1,0:T(8,128)(2,1)S(1)} async-done(((bf16[4,2,8,2048]{3,2,1,0:T(8,128)(2,1)}), bf16[4,2,8,2048]{3,2,1,0:T(8,128)(2,1)S(1)}, u32[]{:S(2)}, u32[]{:S(2)}) %all-to-all-start.9) | async-done | bytes 262176 | tf_op jit(solution)/shard_map/all_to_all | solution.py:59
  331.9 1.2 gather_fusion.9
  (117 shorter events, 25.1 us)
Async XLA Ops:
  6.5 15.6 %copy-start = (bf16[4,8,2048]{2,1,0:T(8,128)(2,1)S(1)}, bf16[4,8,2048]{2,1,0:T(8,128)(2,1)}, u32[]{:S(2)}) copy-start(bf16[4,8,2048]{2,1,0:T(8,128)(2,1)} %param.9) | copy-start | bytes 393220
  6.5 58.7 %all-gather.11.cloned.1.call-start = ((), (), s32[]{:S(2)}) async-start(), calls=%async_computation.11 | async-start | bytes 7864320 | tf_op jit(solution)/shard_map/all_gather | solution.py:14
  13.1 135.9 %all-gather.9.cloned.1.call-start = ((), (), s32[]{:S(2)}) async-start(), calls=%async_computation.10 | async-start | bytes 15728640 | tf_op jit(solution)/shard_map/all_gather | solution.py:14
  19.0 1.3 copy-start.6
  19.0 195.3 %all-gather.15.cloned.1.call-start = ((), (), s32[]{:S(2)}) async-start(), calls=%async_computation.13 | async-start | bytes 7864320 | tf_op jit(solution)/shard_map/all_gather | solution.py:14
  19.1 8.6 %copy-start.7 = (s32[2,64,1]{1,2,0:T(1,128)S(1)}, s32[2,64,1]{1,2,0:T(1,128)}, u32[]{:S(2)}) copy-start(s32[2,64,1]{1,2,0:T(1,128)} %param.16) | copy-start | bytes 1540
  19.1 10.0 %copy-start.5 = (f32[2,2048]{1,0:T(2,128)S(1)}, f32[2,2048]{1,0:T(2,128)}, u32[]{:S(2)}) copy-start(f32[2,2048]{1,0:T(2,128)} %param.15) | copy-start | bytes 49156
  19.8 263.5 %all-gather.13.cloned.1.call-start = ((), (), s32[]{:S(2)}) async-start(), calls=%async_computation.12 | async-start | bytes 15728640 | tf_op jit(solution)/shard_map/all_gather | solution.py:14
  20.8 1.3 copy-start.9
  23.5 13.4 %all-to-all-start = ((bf16[4,2,8,2048]{3,2,1,0:T(8,128)(2,1)}), bf16[4,2,8,2048]{3,2,1,0:T(8,128)(2,1)S(1)}, u32[]{:S(2)}, u32[]{:S(2)}) async-start(bf16[4,2,8,2048]{3,2,1,0:T(8,128)(2,1)} %broadcast_select_fusion.6), calls=%async_computation | async-start | bytes 524288 | tf_op jit(solution)/shard_map/all_to_all | solution.py:50
  37.2 8.4 %copy-start.2 = (s32[4]{0:T(128)S(1)}, s32[4]{0:T(128)}, u32[]{:S(2)}) copy-start(s32[4]{0:T(128)} %param.10) | copy-start | bytes 52
  39.2 20.7 %all-to-all-start.2 = ((bf16[8,10,2048]{2,1,0:T(8,128)(2,1)}), bf16[8,10,2048]{2,1,0:T(8,128)(2,1)S(1)}, u32[]{:S(2)}, u32[]{:S(2)}) async-start(bf16[8,10,2048]{2,1,0:T(8,128)(2,1)} %broadcast_select_fusion.5), calls=%async_computation.2 | async-start | bytes 1048576 | tf_op jit(solution)/shard_map/all_to_all | solution.py:90
  59.9 100.8 %all-to-all-start.1 = ((s32[4,2,1]{1,2,0:T(1,128)}), s32[4,2,1]{1,2,0:T(1,128)S(1)}, u32[]{:S(2)}, u32[]{:S(2)}) async-start(s32[4,2,1]{1,2,0:T(1,128)} %bitcast.9), calls=%async_computation.1 | async-start | bytes 4096 | tf_op jit(solution)/shard_map/all_to_all | solution.py:51
  157.6 1.8 copy-start.4
  157.6 8.6 %copy-start.8 = (f32[2,64]{1,0:T(2,128)S(1)}, f32[2,64]{1,0:T(2,128)}, u32[]{:S(2)}) copy-start(f32[2,64]{1,0:T(2,128)} %param.17) | copy-start | bytes 1540
  160.7 20.4 %all-to-all-start.3 = ((bf16[8,10,2048]{2,1,0:T(8,128)(2,1)}), bf16[8,10,2048]{2,1,0:T(8,128)(2,1)S(1)}, u32[]{:S(2)}, u32[]{:S(2)}) async-start(bf16[8,10,2048]{2,1,0:T(8,128)(2,1)} %reshape.332), calls=%async_computation.3 | async-start | bytes 1048576 | tf_op jit(solution)/shard_map/all_to_all | solution.py:97
  182.8 12.5 %all-to-all-start.4 = ((bf16[4,2,8,2048]{3,2,1,0:T(8,128)(2,1)}), bf16[4,2,8,2048]{3,2,1,0:T(8,128)(2,1)S(1)}, u32[]{:S(2)}, u32[]{:S(2)}) async-start(bf16[4,2,8,2048]{3,2,1,0:T(8,128)(2,1)} %fusion.3), calls=%async_computation.4 | async-start | bytes 524288 | tf_op jit(solution)/shard_map/all_to_all | solution.py:59
  197.3 9.4 %all-to-all-start.5 = ((bf16[4,2,8,2048]{3,2,1,0:T(8,128)(2,1)}), bf16[4,2,8,2048]{3,2,1,0:T(8,128)(2,1)S(1)}, u32[]{:S(2)}, u32[]{:S(2)}) async-start(bf16[4,2,8,2048]{3,2,1,0:T(8,128)(2,1)} %broadcast_select_fusion.7), calls=%async_computation.5 | async-start | bytes 524288 | tf_op jit(solution)/shard_map/all_to_all | solution.py:50
  208.9 83.0 %all-to-all-start.7 = ((bf16[8,10,2048]{2,1,0:T(8,128)(2,1)}), bf16[8,10,2048]{2,1,0:T(8,128)(2,1)}, u32[]{:S(2)}, u32[]{:S(2)}) async-start(bf16[8,10,2048]{2,1,0:T(8,128)(2,1)} %broadcast_select_fusion.4), calls=%async_computation.7 | async-start | bytes 1048576 | tf_op jit(solution)/shard_map/all_to_all | solution.py:90
  291.9 8.2 %all-to-all-start.6 = ((s32[4,2,1]{1,2,0:T(1,128)}), s32[4,2,1]{1,2,0:T(1,128)S(1)}, u32[]{:S(2)}, u32[]{:S(2)}) async-start(s32[4,2,1]{1,2,0:T(1,128)} %bitcast.21), calls=%async_computation.6 | async-start | bytes 4096 | tf_op jit(solution)/shard_map/all_to_all | solution.py:51
  297.0 1.7 copy-start.3
  299.2 33.9 %copy-start.1 = (bf16[4,8,2048]{2,1,0:T(8,128)(2,1)S(1)}, bf16[4,8,2048]{2,1,0:T(8,128)(2,1)}, u32[]{:S(2)}) copy-start(bf16[4,8,2048]{2,1,0:T(8,128)(2,1)} %param.9) | copy-start | bytes 393220
  300.1 20.6 %all-to-all-start.8 = ((bf16[8,10,2048]{2,1,0:T(8,128)(2,1)}), bf16[8,10,2048]{2,1,0:T(8,128)(2,1)S(1)}, u32[]{:S(2)}, u32[]{:S(2)}) async-start(bf16[8,10,2048]{2,1,0:T(8,128)(2,1)} %reshape.337), calls=%async_computation.8 | async-start | bytes 1048576 | tf_op jit(solution)/shard_map/all_to_all | solution.py:97
  322.5 9.4 %all-to-all-start.9 = ((bf16[4,2,8,2048]{3,2,1,0:T(8,128)(2,1)}), bf16[4,2,8,2048]{3,2,1,0:T(8,128)(2,1)S(1)}, u32[]{:S(2)}, u32[]{:S(2)}) async-start(bf16[4,2,8,2048]{3,2,1,0:T(8,128)(2,1)} %fusion.1), calls=%async_computation.9 | async-start | bytes 524288 | tf_op jit(solution)/shard_map/all_to_all | solution.py:59
Sparse Core Ops, SparseCore 0:
  13.2 52.0 all-gather.10
  66.8 82.0 all-gather.8
  150.5 49.1 all-gather.14
  201.2 82.0 all-gather.12
